TPU v7x, 256 devices: a whole 4x4x8 slice. The times are simulated.
256 devices in a mesh: member: 64 (over z, x, core), dp: 4 (over y).
Axes of the slice: x: 4, y: 4, z: 8, core: 2. Of those that a mesh axis runs over, the one named last changes fastest.
Arguments:
- feature_pool: bfloat16 [2048, 256], P('dp'), may hold values from -6 to 6
- labels: int32 [2048], P('dp'), may hold values from 0 to 9
- sample_rows: int32 [1024], P('dp'), may hold values from 0 to 511
- noise_variance: float32 [10], replicated, may hold values from 20 to 80
- first_weight: bfloat16 [128, 256, 2048], P('member', None, 'dp'), may hold values from -6 to 6
- middle_weight: bfloat16 [128, 2048, 2048], P('member', 'dp'), may hold values from -6 to 6
- last_weight: bfloat16 [128, 2048, 10], P('member', 'dp'), may hold values from -6 to 6
Outputs:
- new_first: bfloat16 [128, 256, 2048], P('member', None, 'dp')
- new_middle: bfloat16 [128, 2048, 2048], P('member', 'dp')
- new_last: bfloat16 [128, 2048, 10], P('member', 'dp')
Inputs may be any that keep to these rules, and one draw needn't show every extreme that they name: Sample i reads pool row (i // 256) * 512 + sample_rows[i]. `labels`: class index of each pool row.
All inputs are finite; a program needn't handle non-finite values.
Results may differ from a plain program's by a relative error of at most 0.013.
Values may be sent and summed in bfloat16 or wider, within the bound.
A program may use at most 128 MiB of HBM per device.

v0:
```python
import jax
import jax.numpy as jnp
from jax import lax
from jax.sharding import PartitionSpec as P

F_IN = 256
H = 2048
precise = lax.Precision.HIGHEST


def from_everyone(x, axis):
    size = lax.axis_size(axis)
    return lax.all_to_all(jnp.broadcast_to(x[None], (size, *x.shape)), axis, 0, 0, tiled=True)


def in_order(parts, dim):
    shape = list(parts.shape[1:])
    shape[dim] *= parts.shape[0]
    return jnp.moveaxis(parts, 0, dim).reshape(shape)


def gathered_copies(x, axis, dim):
    parts = from_everyone(x, axis)
    return in_order(parts, dim)


def side_by_side(arrays, axis, split_dim, concat_dim, along):
    widths = [a.shape[along] for a in arrays]
    both = jnp.concatenate(arrays, axis=along)
    filled = lax.all_to_all(both, axis, split_axis=split_dim, concat_axis=concat_dim, tiled=True)
    return tuple(jnp.split(filled, [sum(widths[:k]) for k in range(1, len(widths))], axis=along))


def update_piece(piece, mixing):
    ensemble = piece.shape[0]
    flat = piece.reshape(ensemble, -1)
    upper = mixing.astype(jnp.bfloat16)
    lower = (mixing - upper.astype(jnp.float32)).astype(jnp.bfloat16)
    stacked = jnp.concatenate([upper.T, lower.T], axis=0)
    both = jnp.dot(stacked, flat, preferred_element_type=jnp.float32)
    product = both[:ensemble] + both[ensemble:]
    column_total = jnp.sum(mixing, axis=0)
    average = jnp.sum(flat, axis=0, dtype=jnp.float32) / ensemble
    renewed = flat.astype(jnp.float32) + product - column_total[:, None] * average[None, :]
    return renewed.astype(jnp.bfloat16).reshape(piece.shape)


def on_device(
    feature_pool, labels, sample_rows, noise_variance, first_weight, middle_weight, last_weight
):
    local_count = sample_rows.shape[0]
    members_here = first_weight.shape[0]
    classes_total = noise_variance.shape[0]
    in_scale = F_IN ** (-0.5)
    hid_scale = H ** (-0.5)
    inputs = feature_pool[sample_rows]
    classes = labels[sample_rows]
    target = (classes[:, None] == jnp.arange(classes_total, dtype=jnp.int32)[None, :]).astype(
        jnp.float32
    )
    window = gathered_copies(inputs, "dp", 0)
    hidden_one = jnp.tanh(
        jnp.einsum("sf,jfh->jsh", window, first_weight, preferred_element_type=jnp.float32)
        * in_scale
    ).astype(jnp.bfloat16)
    term = jnp.einsum("jsk,jkh->sjh", hidden_one, middle_weight, preferred_element_type=jnp.float32)
    summed = lax.psum_scatter(
        term.reshape(lax.axis_size("dp") * local_count, members_here * H).astype(jnp.bfloat16),
        "dp",
        scatter_dimension=0,
        tiled=True,
    ).astype(jnp.float32)
    hidden_two = jnp.tanh(summed.reshape(local_count, members_here, H) * hid_scale).astype(
        jnp.bfloat16
    )
    last_full = lax.all_gather(last_weight, "dp", axis=1, tiled=True)
    outputs = (
        jnp.einsum("sjh,jhc->jsc", hidden_two, last_full, preferred_element_type=jnp.float32)
        * hid_scale
    )
    whiten = 1.0 / jnp.sqrt(noise_variance)
    scaled = (outputs * whiten).reshape(members_here, local_count * classes_total)
    observed = (target * whiten).reshape(local_count * classes_total)
    every_member = lax.all_gather(scaled, "member", axis=0, tiled=True)
    center = jnp.mean(every_member, axis=0)
    anomaly = every_member - center
    gram_part = jnp.dot(anomaly, anomaly.T, precision=precise)
    drive_part = jnp.dot(anomaly, observed - center, precision=precise)
    gram_matrix, drive = (
        lax.psum(gram_part.astype(jnp.bfloat16), "dp").astype(jnp.float32),
        lax.psum(drive_part.astype(jnp.bfloat16), "dp").astype(jnp.float32),
    )
    ensemble = gram_matrix.shape[0]
    system = gram_matrix + ensemble * jnp.eye(ensemble, dtype=jnp.float32)
    factor = jnp.linalg.cholesky(system)
    mixing = jax.scipy.linalg.cho_solve((factor, True), drive[:, None] - gram_matrix)
    grouped = (
        lax.all_to_all(first_weight, "member", split_axis=1, concat_axis=0, tiled=True),
        *side_by_side((middle_weight, last_weight), "member", 1, 0, 2),
    )
    updated = (
        update_piece(grouped[0], mixing),
        update_piece(grouped[1], mixing),
        update_piece(grouped[2], mixing),
    )
    new_first, new_middle, new_last = (
        lax.all_to_all(updated[0], "member", split_axis=0, concat_axis=1, tiled=True),
        *side_by_side((updated[1], updated[2]), "member", 0, 1, 2),
    )
    return (new_first, new_middle, new_last)


def solution(mesh):
    in_specs = (
        P("dp", None),
        P("dp"),
        P("dp"),
        P(),
        P("member", None, "dp"),
        P("member", "dp", None),
        P("member", "dp", None),
    )
    out_specs = (P("member", None, "dp"), P("member", "dp", None), P("member", "dp", None))
    return jax.shard_map(
        on_device, mesh=mesh, in_specs=in_specs, out_specs=out_specs, check_vma=False
    )
```

profile of v0, /device:TPU:2, one launch (start us, length us, event | category | flops | bytes accessed | tf_op | source)
XLA Modules:
  0.0 416.6 jit_solution(17062474247449413385)
XLA Ops:
  9.3 13.7 %all_to_all.74 = bf16[4,256,256]{2,1,0:T(8,128)(2,1)S(1)} all-to-all(bf16[4,256,256]{2,1,0:T(8,128)(2,1)S(1)} %broadcast_in_dim.6), channel_id=1, replica_groups=mesh['member'=64,'dp'=4] {'dp'}, dimensions={0} | all-to-all | bytes 1048576 | tf_op jit(solution)/shard_map/all_to_all | solution.py:13
  23.1 9.5 %convert_bitcast_fusion = bf16[1024,2,2048]{2,0,1:T(8,128)(2,1)} fusion(bf16[2,512,2048]{2,1,0:T(8,128)(2,1)} %param.12, bf16[1024,256,1]{1,0,2:T(8,128)(2,1)S(1)} %bitcast.96, bf16[2,256,512]{2,1,0:T(8,128)(2,1)} %param.11), kind=kOutput, calls=%fused_computation.7 | convolution fusion | flops 4838129664 | bytes 13631488 | tf_op jit(solution)/shard_map/jsk,jkh->sjh/dot_general | solution.py:66
  32.5 11.9 %copy.78 = bf16[1024,2,2048]{0,2,1:T(8,128)(2,1)} copy(bf16[1024,2,2048]{2,0,1:T(8,128)(2,1)} %convert_bitcast_fusion) | data formatting | bytes 16777216 | tf_op jit(solution)/shard_map/convert_element_type | solution.py:68
  46.8 12.4 %all-to-all-start = ((bf16[2,256,512]{2,0,1:T(2,128)(2,1)}), bf16[2,256,512]{2,0,1:T(2,128)(2,1)S(1)}, u32[]{:S(2)}, u32[]{:S(2)}) async-start(bf16[2,256,512]{2,0,1:T(2,128)(2,1)} %copy.76), calls=%async_computation | async-start | bytes 1048576 | tf_op jit(solution)/shard_map/all_to_all | solution.py:98
  59.2 8.5 %copy.84 = bf16[2,512,2048]{2,0,1:T(2,128)(2,1)} copy(bf16[2,512,2048]{2,1,0:T(8,128)(2,1)} %param.12) | data formatting | bytes 8388608 | tf_op args[5]
  67.9 8.4 %pad_maximum_fusion = bf16[2,512,2058]{2,0,1:T(2,128)(2,1)} fusion(bf16[2,512,10]{2,0,1:T(2,128)(2,1)S(1)} %copy.85, bf16[2,512,2048]{2,0,1:T(2,128)(2,1)} %copy.84), kind=kLoop, calls=%fused_computation.8 | loop fusion | flops 8429568 | bytes 8429568 | tf_op jit(solution)/shard_map/concatenate | solution.py:29
  76.6 10.3 %all-to-all-start.3 = ((bf16[2,512,2058]{2,0,1:T(2,128)(2,1)}), bf16[2,512,2058]{2,0,1:T(2,128)(2,1)}, u32[]{:S(2)}, u32[]{:S(2)}) async-start(bf16[2,512,2058]{2,0,1:T(2,128)(2,1)} %pad_maximum_fusion), calls=%async_computation.4 | async-start | bytes 8912896 | tf_op jit(solution)/shard_map/all_to_all | solution.py:30
  87.0 13.2 %all_gather.6 = bf16[2,2048,10]{1,2,0:T(8,128)(2,1)S(1)} all-gather(bf16[2,512,10]{1,2,0:T(8,128)(2,1)S(1)} %copy.79), channel_id=1, replica_groups=mesh['member'=64,'dp'=4] {'dp'}, dimensions={1}, use_global_device_ids=true | all-gather | bytes 102400 | tf_op jit(solution)/shard_map/all_gather | solution.py:76
  100.1 29.5 %reduce-scatter.2.cloned.1.call-done = bf16[256,4096]{0,1:T(8,128)(2,1)} async-done(((bf16[1024,4096]{0,1:T(8,128)(2,1)}), bf16[256,4096]{0,1:T(8,128)(2,1)}) %reduce-scatter.2.cloned.1.call-update) | async-done | bytes 2097168 | tf_op jit(solution)/shard_map/reduce_scatter | solution.py:67
  136.0 53.5 %all-to-all-done.3 = bf16[2,512,2058]{2,0,1:T(2,128)(2,1)} async-done(((bf16[2,512,2058]{2,0,1:T(2,128)(2,1)}), bf16[2,512,2058]{2,0,1:T(2,128)(2,1)}, u32[]{:S(2)}, u32[]{:S(2)}) %all-to-all-start.3) | async-done | bytes 4214816 | tf_op jit(solution)/shard_map/all_to_all | solution.py:30
  189.4 3.0 copy.86
  192.5 3.0 split.16
  196.1 2.8 convert_reduce_fusion
  199.1 7.3 %copy.95 = bf16[16,8,8,2048]{3,1,2,0:T(8,128)(2,1)} copy(bf16[16,8,8,2048]{3,2,1,0:T(8,128)(2,1)} %bitcast.85) | data formatting | bytes 8388608
  206.5 11.1 %all-gather.3.cloned.1.call-done = f32[64,2,2560]{2,1,0:T(2,128)} async-done(((f32[1,2,2560]{2,1,0:T(2,128)}), f32[64,2,2560]{2,1,0:T(2,128)}) %all-gather.3.cloned.1.call-update) | async-done | bytes 1310736 | tf_op jit(solution)/shard_map/all_gather | solution.py:84
  223.9 17.5 %all-reduce = (bf16[128,128]{1,0:T(8,128)(2,1)S(1)}, bf16[128]{0:T(256)(128)(2,1)S(1)}) all-reduce(bf16[128,128]{1,0:T(8,128)(2,1)S(1)} %fusion.8, bf16[128]{0:T(256)(128)(2,1)S(1)} %fusion.14), channel_id=1, replica_groups=mesh['member'=64,'dp'=4] {'dp'}, use_global_device_ids=true, to_apply=%region_2.0 | all-reduce | flops 16512 | bytes 66048 | tf_op jit(solution)/shard_map/psum | solution.py:90
  241.6 11.7 %cholesky.16 = f32[128,128]{1,0:T(8,128)S(1)} custom-call(f32[128,128]{1,0:T(8,128)S(1)} %fusion.29), custom_call_target="Cholesky" | custom-call | tf_op jit(solution)/shard_map/jit(cholesky)/cholesky | solution.py:95
  254.7 9.8 %custom-call.10 = f32[1,128,128]{1,2,0:T(8,128)S(1)} custom-call(f32[1,128,128]{2,1,0:T(8,128)S(1)} %fusion.23), custom_call_target="InvertDiagBlocksLowerTriangular" | custom-call | tf_op jit(solution)/shard_map/jit(_cho_solve)/triangular_solve | solution.py:96
  267.0 8.2 %all-to-all-start.2 = ((bf16[128,4,512]{2,1,0:T(4,128)(2,1)}), bf16[128,4,512]{2,1,0:T(4,128)(2,1)S(1)}, u32[]{:S(2)}, u32[]{:S(2)}) async-start(bf16[128,4,512]{2,1,0:T(4,128)(2,1)} %reshape.97), calls=%async_computation.3 | async-start | bytes 1048576 | tf_op jit(solution)/shard_map/all_to_all | solution.py:107
  275.2 4.7 %fusion.35 = f32[256,16384]{1,0:T(8,128)S(1)} fusion(bf16[128,16384]{1,0:T(8,128)(2,1)} %bitcast.80, bf16[128,128]{0,1:T(8,128)(2,1)S(1)} %get-tuple-element.29, bf16[128,128]{0,1:T(8,128)(2,1)S(1)} %get-tuple-element.24), kind=kOutput, calls=%fused_computation.57 | convolution fusion | flops 1073872896 | bytes 21037056 | tf_op jit(solution)/shard_map/dot_general | solution.py:40
  280.0 3.3 fusion.2
  283.8 5.0 %copy.97 = bf16[16,8,8,2048]{3,2,1,0:T(8,128)(2,1)S(1)} copy(bf16[16,8,8,2048]{3,1,2,0:T(8,128)(2,1)} %bitcast.87) | data formatting | bytes 8388608
  292.7 9.1 %all-to-all-start.4 = ((bf16[128,8,2058]{2,1,0:T(8,128)(2,1)}), bf16[128,8,2058]{2,1,0:T(8,128)(2,1)}, u32[]{:S(2)}, u32[]{:S(2)}) async-start(bf16[128,8,2058]{2,1,0:T(8,128)(2,1)} %pad_maximum_fusion.1), calls=%async_computation.5 | async-start | bytes 8912896 | tf_op jit(solution)/shard_map/all_to_all | solution.py:30
  302.9 100.7 %all-to-all-done.4 = bf16[128,8,2058]{2,1,0:T(8,128)(2,1)} async-done(((bf16[128,8,2058]{2,1,0:T(8,128)(2,1)}), bf16[128,8,2058]{2,1,0:T(8,128)(2,1)}, u32[]{:S(2)}, u32[]{:S(2)}) %all-to-all-start.4) | async-done | bytes 4214816 | tf_op jit(solution)/shard_map/all_to_all | solution.py:30
  (80 shorter events, 33.9 us)
Async XLA Ops:
  7.2 1.0 copy-start
  7.2 122.4 %reduce-scatter.2.cloned.1.call-start = ((), (), s32[]{:S(2)}) async-start(), calls=%async_computation.6 | async-start | bytes 10485760 | tf_op jit(solution)/shard_map/reduce_scatter | solution.py:67
  44.4 1.0 copy-start.5
  46.8 29.9 %all-to-all-start = ((bf16[2,256,512]{2,0,1:T(2,128)(2,1)}), bf16[2,256,512]{2,0,1:T(2,128)(2,1)S(1)}, u32[]{:S(2)}, u32[]{:S(2)}) async-start(bf16[2,256,512]{2,0,1:T(2,128)(2,1)} %copy.76), calls=%async_computation | async-start | bytes 1048576 | tf_op jit(solution)/shard_map/all_to_all | solution.py:98
  59.2 8.5 %copy-start.6 = (bf16[2,512,10]{1,0,2:T(2,128)(2,1)S(1)}, bf16[2,512,10]{1,0,2:T(2,128)(2,1)}, u32[]{:S(2)}) copy-start(bf16[2,512,10]{1,0,2:T(2,128)(2,1)} %param.13) | copy-start | bytes 61444
  76.3 23.8 %copy-start.7 = (f32[10]{0:T(128)S(1)}, f32[10]{0:T(128)}, u32[]{:S(2)}) copy-start(f32[10]{0:T(128)} %param.10) | copy-start | bytes 124
  76.6 112.8 %all-to-all-start.3 = ((bf16[2,512,2058]{2,0,1:T(2,128)(2,1)}), bf16[2,512,2058]{2,0,1:T(2,128)(2,1)}, u32[]{:S(2)}, u32[]{:S(2)}) async-start(bf16[2,512,2058]{2,0,1:T(2,128)(2,1)} %pad_maximum_fusion), calls=%async_computation.4 | async-start | bytes 8912896 | tf_op jit(solution)/shard_map/all_to_all | solution.py:30
  86.9 46.2 %copy-start.2 = (s32[512]{0:T(512)S(1)}, s32[512]{0:T(512)}, u32[]{:S(2)}) copy-start(s32[512]{0:T(512)} %param.8) | copy-start | bytes 6148
  86.9 130.7 %all-gather.3.cloned.1.call-start = ((), (), s32[]{:S(2)}) async-start(), calls=%async_computation.7 | async-start | bytes 1331200 | tf_op jit(solution)/shard_map/all_gather | solution.py:84
  192.5 3.4 copy-start.3
  267.0 25.7 %all-to-all-start.2 = ((bf16[128,4,512]{2,1,0:T(4,128)(2,1)}), bf16[128,4,512]{2,1,0:T(4,128)(2,1)S(1)}, u32[]{:S(2)}, u32[]{:S(2)}) async-start(bf16[128,4,512]{2,1,0:T(4,128)(2,1)} %reshape.97), calls=%async_computation.3 | async-start | bytes 1048576 | tf_op jit(solution)/shard_map/all_to_all | solution.py:107
  275.2 4.7 %copy-start.4 = (bf16[16,8,8,2048]{3,1,2,0:T(8,128)(2,1)S(1)}, bf16[16,8,8,2048]{3,1,2,0:T(8,128)(2,1)}, u32[]{:S(2)}) copy-start(bf16[16,8,8,2048]{3,1,2,0:T(8,128)(2,1)} %copy.95) | copy-start | bytes 12582916
  292.7 110.9 %all-to-all-start.4 = ((bf16[128,8,2058]{2,1,0:T(8,128)(2,1)}), bf16[128,8,2058]{2,1,0:T(8,128)(2,1)}, u32[]{:S(2)}, u32[]{:S(2)}) async-start(bf16[128,8,2058]{2,1,0:T(8,128)(2,1)} %pad_maximum_fusion.1), calls=%async_computation.5 | async-start | bytes 8912896 | tf_op jit(solution)/shard_map/all_to_all | solution.py:30
  406.1 3.4 copy-start.1
Sparse Core Ops, SparseCore 0:
  44.5 85.0 reduce-scatter.1
  133.2 84.3 all-gather.2
where the time goes:
time: 422 us; the launch traced here: 417 us
  waiting for transfers between devices  196 us (46%)
  local copies, waits for them, and re-layouts  57.5 us (14%)
  other arithmetic  45.5 us (11%)
  blocking collectives  44.4 us (11%)
  starting transfers between devices  40.1 us (10%)
  matrix products  18 us (4%)
  between operations  14.6 us (3%)
    all_to_all x2, waiting for transfers between devices, side_by_side(): lax.all_to_all(both, axis, split_axis=split_dim, concat_axis=concat_dim,...  154 us
    reduce_scatter x1, waiting for transfers between devices, on_device(): lax.psum_scatter(term.reshape(lax.axis_size('dp') * local_count, members_...  29.5 us
    unnamed x28, local copies, waits for them, and re-layouts  27.9 us
    all_to_all x2, starting transfers between devices, side_by_side(): lax.all_to_all(both, axis, split_axis=split_dim, concat_axis=concat_dim,...  19.4 us
    psum x1, blocking collectives, on_device(): lax.psum(gram_part.astype(jnp.bfloat16), 'dp').astype(jnp.float32)  17.5 us
    all_to_all x1, blocking collectives, from_everyone(): lax.all_to_all(jnp.broadcast_to(x[None], (size, *x.shape)), axis, 0, 0, t...  13.7 us
    all_gather x1, blocking collectives, on_device(): last_full = lax.all_gather(last_weight, 'dp', axis=1, tiled=True)  13.2 us
    all_to_all x1, starting transfers between devices, on_device(): lax.all_to_all(first_weight, 'member', split_axis=1, concat_axis=0, tiled...  12.4 us
  transfers between devices with their start and end apart: 6, of which 6 were waited for; matrix products, arithmetic and copies ran while one was open for 14% of the time, Pallas kernels for 0%

commit v1 on v0

--- a/solution.py
+++ b/solution.py
@@ -6,6 +6,22 @@
 F_IN = 256
 H = 2048
 precise = lax.Precision.HIGHEST
+
+
+def ring_product(value, axis, dim, contribution):
+    devices, place, width = (lax.axis_size(axis), lax.axis_index(axis), value.shape[dim])
+    right = [(i, (i + 1) % devices) for i in range(devices)]
+    left = [(i, (i - 1) % devices) for i in range(devices)]
+    halfway = devices // 2
+    from_left = from_right = value
+    running = contribution(value, place * width)
+    for step in range(1, halfway + 1):
+        from_left = lax.ppermute(from_left, axis, right)
+        if step < devices - halfway:
+            from_right = lax.ppermute(from_right, axis, left)
+            running = running + contribution(from_right, (place + step) % devices * width)
+        running = running + contribution(from_left, (place - step) % devices * width)
+    return running
 
 
 def from_everyone(x, axis):
@@ -73,9 +89,18 @@
     hidden_two = jnp.tanh(summed.reshape(local_count, members_here, H) * hid_scale).astype(
         jnp.bfloat16
     )
-    last_full = lax.all_gather(last_weight, "dp", axis=1, tiled=True)
     outputs = (
-        jnp.einsum("sjh,jhc->jsc", hidden_two, last_full, preferred_element_type=jnp.float32)
+        ring_product(
+            last_weight,
+            "dp",
+            1,
+            lambda part, start: jnp.einsum(
+                "sjh,jhc->jsc",
+                lax.dynamic_slice_in_dim(hidden_two, start, part.shape[1], axis=2),
+                part,
+                preferred_element_type=jnp.float32,
+            ),
+        )
         * hid_scale
     )
     whiten = 1.0 / jnp.sqrt(noise_variance)

time: 422 us -> 422 us (level)
  blocking collectives: 44.4 us -> 31.3 us
  waiting for transfers between devices: 196 us -> 207 us
    all_gather x1 -> x0, blocking collectives: 13.2 us -> none  [on_device(): last_full = lax.all_gather(last_weight, 'dp', axis=1, tiled=True)]
    reduce_scatter x1, waiting for transfers between devices: 29.5 us -> 35.4 us  [on_device(): lax.psum_scatter(term.reshape(lax.axis_size('dp') * local_count, members_...]
    ppermute x0 -> x3, waiting for transfers between devices: none -> 5.08 us  [the longest x2 5.07 us: ring_product(): from_left = lax.ppermute(from_left, axis, right)]
  transfers between devices with their start and end apart: 6 -> 9, of which waited for: 6 -> 7; matrix products, arithmetic and copies ran while one was open for 14% -> 14% of each run, Pallas kernels for 0% -> 0%
where the time goes in v1:
time: 422 us; the launch traced here: 417 us
  waiting for transfers between devices  207 us (49%)
  local copies, waits for them, and re-layouts  57.5 us (14%)
  other arithmetic  45.5 us (11%)
  starting transfers between devices  42.7 us (10%)
  blocking collectives  31.3 us (7%)
  matrix products  18.3 us (4%)
  between operations  14.7 us (3%)
    all_to_all x2, waiting for transfers between devices, side_by_side(): lax.all_to_all(both, axis, split_axis=split_dim, concat_axis=concat_dim,...  154 us
    reduce_scatter x1, waiting for transfers between devices, on_device(): lax.psum_scatter(term.reshape(lax.axis_size('dp') * local_count, members_...  35.4 us
    unnamed x28, local copies, waits for them, and re-layouts  27.8 us
    all_to_all x2, starting transfers between devices, side_by_side(): lax.all_to_all(both, axis, split_axis=split_dim, concat_axis=concat_dim,...  19.4 us
    psum x1, blocking collectives, on_device(): lax.psum(gram_part.astype(jnp.bfloat16), 'dp').astype(jnp.float32)  17.6 us
    all_to_all x1, blocking collectives, from_everyone(): lax.all_to_all(jnp.broadcast_to(x[None], (size, *x.shape)), axis, 0, 0, t...  13.7 us
    all_to_all x1, starting transfers between devices, on_device(): lax.all_to_all(first_weight, 'member', split_axis=1, concat_axis=0, tiled...  12.6 us
    another operation x3, other arithmetic, on_device(): factor = jnp.linalg.cholesky(system)  12.4 us
  transfers between devices with their start and end apart: 9, of which 7 were waited for; matrix products, arithmetic and copies ran while one was open for 14% of the time, Pallas kernels for 0%

profile of v1, /device:TPU:2, one launch (start us, length us, event | category | flops | bytes accessed | tf_op | source)
XLA Modules:
  0.0 416.9 jit_solution(664232557215063313)
XLA Ops:
  9.3 13.7 %all_to_all.74 = bf16[4,256,256]{2,1,0:T(8,128)(2,1)S(1)} all-to-all(bf16[4,256,256]{2,1,0:T(8,128)(2,1)S(1)} %broadcast_in_dim.6), channel_id=1, replica_groups=mesh['member'=64,'dp'=4] {'dp'}, dimensions={0} | all-to-all | bytes 1048576 | tf_op jit(solution)/shard_map/all_to_all | solution.py:29
  23.1 9.5 %convert_bitcast_fusion = bf16[1024,2,2048]{2,0,1:T(8,128)(2,1)} fusion(bf16[2,512,2048]{2,1,0:T(8,128)(2,1)} %param.12, bf16[1024,256,1]{1,0,2:T(8,128)(2,1)S(1)} %bitcast.100, bf16[2,256,512]{2,1,0:T(8,128)(2,1)} %param.11), kind=kOutput, calls=%fused_computation.7 | convolution fusion | flops 4838129664 | bytes 13631488 | tf_op jit(solution)/shard_map/jsk,jkh->sjh/dot_general | solution.py:82
  32.5 11.9 %copy.100 = bf16[1024,2,2048]{0,2,1:T(8,128)(2,1)} copy(bf16[1024,2,2048]{2,0,1:T(8,128)(2,1)} %convert_bitcast_fusion) | data formatting | bytes 16777216 | tf_op jit(solution)/shard_map/convert_element_type | solution.py:84
  46.8 12.6 %all-to-all-start = ((bf16[2,256,512]{2,0,1:T(2,128)(2,1)}), bf16[2,256,512]{2,0,1:T(2,128)(2,1)S(1)}, u32[]{:S(2)}, u32[]{:S(2)}) async-start(bf16[2,256,512]{2,0,1:T(2,128)(2,1)} %copy.98), calls=%async_computation | async-start | bytes 1048576 | tf_op jit(solution)/shard_map/all_to_all | solution.py:123
  59.4 8.5 %copy.111 = bf16[2,512,2048]{2,0,1:T(2,128)(2,1)} copy(bf16[2,512,2048]{2,1,0:T(8,128)(2,1)} %param.12) | data formatting | bytes 8388608 | tf_op args[5]
  68.2 8.4 %pad_maximum_fusion = bf16[2,512,2058]{2,0,1:T(2,128)(2,1)} fusion(bf16[2,512,10]{2,0,1:T(2,128)(2,1)S(1)} %copy.112, bf16[2,512,2048]{2,0,1:T(2,128)(2,1)} %copy.111), kind=kLoop, calls=%fused_computation.8 | loop fusion | flops 8429568 | bytes 8429568 | tf_op jit(solution)/shard_map/concatenate | solution.py:45
  76.9 10.3 %all-to-all-start.3 = ((bf16[2,512,2058]{2,0,1:T(2,128)(2,1)}), bf16[2,512,2058]{2,0,1:T(2,128)(2,1)}, u32[]{:S(2)}, u32[]{:S(2)}) async-start(bf16[2,512,2058]{2,0,1:T(2,128)(2,1)} %pad_maximum_fusion), calls=%async_computation.4 | async-start | bytes 8912896 | tf_op jit(solution)/shard_map/all_to_all | solution.py:46
  89.3 5.1 %collective-permute-done.1 = bf16[2,512,10]{1,2,0:T(8,128)(2,1)S(1)} collective-permute-done((bf16[2,512,10]{1,2,0:T(8,128)(2,1)S(1)}, bf16[2,512,10]{1,2,0:T(8,128)(2,1)S(1)}, u32[]{:S(2)}, u32[]{:S(2)}) %collective-permute-start.1) | collective-permute-done | bytes 20512 | tf_op jit(solution)/shard_map/ppermute | solution.py:19
  94.6 35.4 %reduce-scatter.2.cloned.1.call-done = bf16[256,4096]{0,1:T(8,128)(2,1)} async-done(((bf16[1024,4096]{0,1:T(8,128)(2,1)}), bf16[256,4096]{0,1:T(8,128)(2,1)}) %reduce-scatter.2.cloned.1.call-update) | async-done | bytes 2097168 | tf_op jit(solution)/shard_map/reduce_scatter | solution.py:83
  136.7 53.0 %all-to-all-done.3 = bf16[2,512,2058]{2,0,1:T(2,128)(2,1)} async-done(((bf16[2,512,2058]{2,0,1:T(2,128)(2,1)}), bf16[2,512,2058]{2,0,1:T(2,128)(2,1)}, u32[]{:S(2)}, u32[]{:S(2)}) %all-to-all-start.3) | async-done | bytes 4214816 | tf_op jit(solution)/shard_map/all_to_all | solution.py:46
  189.7 3.0 copy.113
  192.7 3.0 split.16
  196.3 2.8 convert_reduce_fusion
  199.3 7.3 %copy.125 = bf16[16,8,8,2048]{3,1,2,0:T(8,128)(2,1)} copy(bf16[16,8,8,2048]{3,2,1,0:T(8,128)(2,1)} %bitcast.86) | data formatting | bytes 8388608
  206.8 11.1 %all-gather.3.cloned.1.call-done = f32[64,2,2560]{2,1,0:T(2,128)} async-done(((f32[1,2,2560]{2,1,0:T(2,128)}), f32[64,2,2560]{2,1,0:T(2,128)}) %all-gather.3.cloned.1.call-update) | async-done | bytes 1310736 | tf_op jit(solution)/shard_map/all_gather | solution.py:109
  224.1 17.6 %all-reduce = (bf16[128,128]{1,0:T(8,128)(2,1)S(1)}, bf16[128]{0:T(256)(128)(2,1)S(1)}) all-reduce(bf16[128,128]{1,0:T(8,128)(2,1)S(1)} %fusion.8, bf16[128]{0:T(256)(128)(2,1)S(1)} %fusion.15), channel_id=1, replica_groups=mesh['member'=64,'dp'=4] {'dp'}, use_global_device_ids=true, to_apply=%region_2.3 | all-reduce | flops 16512 | bytes 66048 | tf_op jit(solution)/shard_map/psum | solution.py:115
  241.8 11.7 %cholesky.16 = f32[128,128]{1,0:T(8,128)S(1)} custom-call(f32[128,128]{1,0:T(8,128)S(1)} %fusion.35), custom_call_target="Cholesky" | custom-call | tf_op jit(solution)/shard_map/jit(cholesky)/cholesky | solution.py:120
  254.9 9.8 %custom-call.10 = f32[1,128,128]{1,2,0:T(8,128)S(1)} custom-call(f32[1,128,128]{2,1,0:T(8,128)S(1)} %fusion.29), custom_call_target="InvertDiagBlocksLowerTriangular" | custom-call | tf_op jit(solution)/shard_map/jit(_cho_solve)/triangular_solve | solution.py:121
  267.2 8.3 %all-to-all-start.2 = ((bf16[128,4,512]{2,1,0:T(4,128)(2,1)}), bf16[128,4,512]{2,1,0:T(4,128)(2,1)S(1)}, u32[]{:S(2)}, u32[]{:S(2)}) async-start(bf16[128,4,512]{2,1,0:T(4,128)(2,1)} %reshape.97), calls=%async_computation.3 | async-start | bytes 1048576 | tf_op jit(solution)/shard_map/all_to_all | solution.py:132
  275.5 4.7 %fusion.41 = f32[256,16384]{1,0:T(8,128)S(1)} fusion(bf16[128,16384]{1,0:T(8,128)(2,1)} %bitcast.81, bf16[128,128]{0,1:T(8,128)(2,1)S(1)} %get-tuple-element.29, bf16[128,128]{0,1:T(8,128)(2,1)S(1)} %get-tuple-element.24), kind=kOutput, calls=%fused_computation.65 | convolution fusion | flops 1073872896 | bytes 21037056 | tf_op jit(solution)/shard_map/dot_general | solution.py:56
  280.2 3.3 fusion.2
  284.0 5.0 %copy.127 = bf16[16,8,8,2048]{3,2,1,0:T(8,128)(2,1)S(1)} copy(bf16[16,8,8,2048]{3,1,2,0:T(8,128)(2,1)} %bitcast.88) | data formatting | bytes 8388608
  292.9 9.1 %all-to-all-start.4 = ((bf16[128,8,2058]{2,1,0:T(8,128)(2,1)}), bf16[128,8,2058]{2,1,0:T(8,128)(2,1)}, u32[]{:S(2)}, u32[]{:S(2)}) async-start(bf16[128,8,2058]{2,1,0:T(8,128)(2,1)} %pad_maximum_fusion.1), calls=%async_computation.5 | async-start | bytes 8912896 | tf_op jit(solution)/shard_map/all_to_all | solution.py:46
  303.1 100.7 %all-to-all-done.4 = bf16[128,8,2058]{2,1,0:T(8,128)(2,1)} async-done(((bf16[128,8,2058]{2,1,0:T(8,128)(2,1)}), bf16[128,8,2058]{2,1,0:T(8,128)(2,1)}, u32[]{:S(2)}, u32[]{:S(2)}) %all-to-all-start.4) | async-done | bytes 4214816 | tf_op jit(solution)/shard_map/all_to_all | solution.py:46
  (88 shorter events, 36.4 us)
Async XLA Ops:
  7.2 1.0 copy-start
  7.2 122.8 %reduce-scatter.2.cloned.1.call-start = ((), (), s32[]{:S(2)}) async-start(), calls=%async_computation.6 | async-start | bytes 10485760 | tf_op jit(solution)/shard_map/reduce_scatter | solution.py:83
  44.4 1.0 copy-start.5
  46.8 30.1 %all-to-all-start = ((bf16[2,256,512]{2,0,1:T(2,128)(2,1)}), bf16[2,256,512]{2,0,1:T(2,128)(2,1)S(1)}, u32[]{:S(2)}, u32[]{:S(2)}) async-start(bf16[2,256,512]{2,0,1:T(2,128)(2,1)} %copy.98), calls=%async_computation | async-start | bytes 1048576 | tf_op jit(solution)/shard_map/all_to_all | solution.py:123
  59.4 8.5 %copy-start.6 = (bf16[2,512,10]{1,0,2:T(2,128)(2,1)S(1)}, bf16[2,512,10]{1,0,2:T(2,128)(2,1)}, u32[]{:S(2)}) copy-start(bf16[2,512,10]{1,0,2:T(2,128)(2,1)} %param.13) | copy-start | bytes 61444
  76.6 12.8 %copy-start.7 = (f32[10]{0:T(128)S(1)}, f32[10]{0:T(128)}, u32[]{:S(2)}) copy-start(f32[10]{0:T(128)} %param.10) | copy-start | bytes 124
  76.9 112.8 %all-to-all-start.3 = ((bf16[2,512,2058]{2,0,1:T(2,128)(2,1)}), bf16[2,512,2058]{2,0,1:T(2,128)(2,1)}, u32[]{:S(2)}, u32[]{:S(2)}) async-start(bf16[2,512,2058]{2,0,1:T(2,128)(2,1)} %pad_maximum_fusion), calls=%async_computation.4 | async-start | bytes 8912896 | tf_op jit(solution)/shard_map/all_to_all | solution.py:46
  87.2 46.7 %copy-start.2 = (s32[512]{0:T(512)S(1)}, s32[512]{0:T(512)}, u32[]{:S(2)}) copy-start(s32[512]{0:T(512)} %param.8) | copy-start | bytes 6148
  87.2 130.7 %all-gather.3.cloned.1.call-start = ((), (), s32[]{:S(2)}) async-start(), calls=%async_computation.7 | async-start | bytes 1331200 | tf_op jit(solution)/shard_map/all_gather | solution.py:109
  87.2 45.1 %collective-permute-start = (bf16[2,512,10]{1,2,0:T(8,128)(2,1)S(1)}, bf16[2,512,10]{1,2,0:T(8,128)(2,1)S(1)}, u32[]{:S(2)}, u32[]{:S(2)}) collective-permute-start(bf16[2,512,10]{1,2,0:T(8,128)(2,1)S(1)} %copy.102), channel_id=1, source_target_pairs={{0,3},{1,0},{2,1},{3,2},{4,7},{5,4},{6,5},{7,6},{8,11},{9,8},{10,9... | collective-permute-start | bytes 61448 | tf_op jit(solution)/shard_map/ppermute | solution.py:21
  88.5 5.9 %collective-permute-start.1 = (bf16[2,512,10]{1,2,0:T(8,128)(2,1)S(1)}, bf16[2,512,10]{1,2,0:T(8,128)(2,1)S(1)}, u32[]{:S(2)}, u32[]{:S(2)}) collective-permute-start(bf16[2,512,10]{1,2,0:T(8,128)(2,1)S(1)} %copy.102), channel_id=1, source_target_pairs={{0,1},{1,2},{2,3},{3,0},{4,5},{5,6},{6,7},{7,4},{8,9},{9,10},{10,1... | collective-permute-start | bytes 61448 | tf_op jit(solution)/shard_map/ppermute | solution.py:19
  94.4 38.3 %collective-permute-start.2 = (bf16[2,512,10]{1,2,0:T(8,128)(2,1)S(1)}, bf16[2,512,10]{1,2,0:T(8,128)(2,1)S(1)}, u32[]{:S(2)}, u32[]{:S(2)}) collective-permute-start(bf16[2,512,10]{1,2,0:T(8,128)(2,1)S(1)} %collective-permute-done.1), channel_id=1, source_target_pairs={{0,1},{1,2},{2,3},{3,0},{4,5},{5,6},{6,7},{7,4},{8,9},{9,10},{10,1... | collective-permute-start | bytes 61448 | tf_op jit(solution)/shard_map/ppermute | solution.py:19
  192.7 3.4 copy-start.3
  267.2 25.7 %all-to-all-start.2 = ((bf16[128,4,512]{2,1,0:T(4,128)(2,1)}), bf16[128,4,512]{2,1,0:T(4,128)(2,1)S(1)}, u32[]{:S(2)}, u32[]{:S(2)}) async-start(bf16[128,4,512]{2,1,0:T(4,128)(2,1)} %reshape.97), calls=%async_computation.3 | async-start | bytes 1048576 | tf_op jit(solution)/shard_map/all_to_all | solution.py:132
  275.5 4.7 %copy-start.4 = (bf16[16,8,8,2048]{3,1,2,0:T(8,128)(2,1)S(1)}, bf16[16,8,8,2048]{3,1,2,0:T(8,128)(2,1)}, u32[]{:S(2)}) copy-start(bf16[16,8,8,2048]{3,1,2,0:T(8,128)(2,1)} %copy.125) | copy-start | bytes 12582916
  292.9 110.9 %all-to-all-start.4 = ((bf16[128,8,2058]{2,1,0:T(8,128)(2,1)}), bf16[128,8,2058]{2,1,0:T(8,128)(2,1)}, u32[]{:S(2)}, u32[]{:S(2)}) async-start(bf16[128,8,2058]{2,1,0:T(8,128)(2,1)} %pad_maximum_fusion.1), calls=%async_computation.5 | async-start | bytes 8912896 | tf_op jit(solution)/shard_map/all_to_all | solution.py:46
  406.4 3.4 copy-start.1
Sparse Core Ops, SparseCore 0:
  44.5 85.3 reduce-scatter.1
  134.0 83.8 all-gather.2
